TPU v7x, 128 devices: a whole 4x4x4 slice. The times are simulated.
128 devices in a mesh: ctx: 32 (over z, y, core), head: 4 (over x).
Axes of the slice: x: 4, y: 4, z: 4, core: 2. Of those that a mesh axis runs over, the one named last changes fastest.
Arguments:
- queries: bfloat16 [32768, 3072], P(('ctx', 'head')), may hold values from -6 to 6
- keys: bfloat16 [32768, 3072], P(('ctx', 'head')), may hold values from -6 to 6
- values: bfloat16 [32768, 3072], P(('ctx', 'head')), may hold values from -6 to 6
- outputs: bfloat16 [32768, 3072], P(('ctx', 'head')), may hold values from -6 to 6
- out_grad: bfloat16 [32768, 3072], P(('ctx', 'head')), may hold values from -4 to 4
- logsumexp: float32 [24, 32768], P('head', 'ctx'), may hold values from 2.5 to 4.5
- clip_of_group: int32 [32], replicated, may hold values from 0 to 15, never falling along the last dimension, each value on 1 to 3 neighbouring positions
Outputs:
- query_grad: bfloat16 [32768, 3072], P(('ctx', 'head'))
- key_grad: bfloat16 [32768, 3072], P(('ctx', 'head'))
- value_grad: bfloat16 [32768, 3072], P(('ctx', 'head'))
Inputs may be any that keep to these rules, and one draw needn't show every extreme that they name: `clip_of_group`: never falls along the groups; each clip holds 1 to 3 consecutive groups, and some clip holds exactly 3.
All inputs are finite; a program needn't handle non-finite values.
Results may differ from a plain program's by a relative error of at most 0.006.
Values may be sent and summed in bfloat16 or wider, within the bound.
A program may use at most 256 MiB of HBM per device.

v0:
```python
import jax
import jax.numpy as jnp
from jax import lax
from jax.sharding import PartitionSpec as P

HD = 128
GROUP = 1024
GROUPS_DEV = 1
SPAN = 2


def passed_along(shard, axis, by):
    count = lax.axis_size(axis)
    pairs = [(i, i + by) for i in range(count) if 0 <= i + by < count]
    return lax.ppermute(shard, axis, pairs)


def tile_grads(query_block, key_block, value_block, grad_block, lse_block, delta_block, visible):
    scale = query_block.shape[-1] ** (-0.5)
    scores = (
        jnp.einsum("qhd,khd->hqk", query_block, key_block, preferred_element_type=jnp.float32)
        * scale
    )
    prob = jnp.where(visible[None], jnp.exp(scores - lse_block[:, :, None]), 0.0)
    prob_b = prob.astype(jnp.bfloat16)
    value_part = jnp.einsum("hqk,qhd->khd", prob_b, grad_block, preferred_element_type=jnp.float32)
    dprob = jnp.einsum("qhd,khd->hqk", grad_block, value_block, preferred_element_type=jnp.float32)
    dscore = (prob * (dprob - delta_block[:, :, None])).astype(jnp.bfloat16)
    query_part = (
        jnp.einsum("hqk,khd->qhd", dscore, key_block, preferred_element_type=jnp.float32) * scale
    )
    key_part = (
        jnp.einsum("hqk,qhd->khd", dscore, query_block, preferred_element_type=jnp.float32) * scale
    )
    return (query_part, key_part, value_part)


def visibility(clip_of_group, query_dev, key_dev, count):
    total = clip_of_group.shape[0]
    query_start = jnp.clip(query_dev * GROUPS_DEV, 0, total - GROUPS_DEV)
    key_start = jnp.clip(key_dev * GROUPS_DEV, 0, total - GROUPS_DEV)
    query_clip = lax.dynamic_slice_in_dim(clip_of_group, query_start, GROUPS_DEV, 0)
    key_clip = lax.dynamic_slice_in_dim(clip_of_group, key_start, GROUPS_DEV, 0)
    offsets = jnp.arange(GROUPS_DEV, dtype=jnp.int32)
    query_index = query_dev * GROUPS_DEV + offsets
    key_index = key_dev * GROUPS_DEV + offsets
    usable = (query_dev >= 0) & (query_dev < count) & (key_dev >= 0) & (key_dev < count)
    group_seen = (
        (query_clip[:, None] == key_clip[None, :])
        & (key_index[None, :] <= query_index[:, None])
        & usable
    )
    rows = GROUPS_DEV * GROUP
    spread = jnp.broadcast_to(group_seen[:, None, :, None], (GROUPS_DEV, GROUP, GROUPS_DEV, GROUP))
    return spread.reshape(rows, rows)


def local(queries, keys, values, outputs, out_grad, logsumexp, clip_of_group):
    heads_local = logsumexp.shape[0]
    query_cols, key_cols, value_cols, output_cols, grad_cols = (
        lax.all_to_all(queries, "head", split_axis=1, concat_axis=0, tiled=True),
        lax.all_to_all(keys, "head", split_axis=1, concat_axis=0, tiled=True),
        lax.all_to_all(values, "head", split_axis=1, concat_axis=0, tiled=True),
        lax.all_to_all(outputs, "head", split_axis=1, concat_axis=0, tiled=True),
        lax.all_to_all(out_grad, "head", split_axis=1, concat_axis=0, tiled=True),
    )
    rows = query_cols.shape[0]
    delta = jnp.einsum(
        "rhd,rhd->hr",
        grad_cols.reshape(rows, heads_local, HD),
        output_cols.reshape(rows, heads_local, HD),
        preferred_element_type=jnp.float32,
    )
    query_heads = query_cols.reshape(rows, heads_local, HD)
    key_heads = key_cols.reshape(rows, heads_local, HD)
    value_heads = value_cols.reshape(rows, heads_local, HD)
    grad_heads = grad_cols.reshape(rows, heads_local, HD)
    device = lax.axis_index("ctx")
    count = lax.axis_size("ctx")
    query_total, key_total, value_total = tile_grads(
        query_heads,
        key_heads,
        value_heads,
        grad_heads,
        logsumexp,
        delta,
        visibility(clip_of_group, device, device, count),
    )
    paired = jnp.stack((key_heads, value_heads))
    for offset in range(1, SPAN + 1):
        remote = passed_along(paired, "ctx", offset)
        query_part, key_part, value_part = tile_grads(
            query_heads,
            remote[0],
            remote[1],
            grad_heads,
            logsumexp,
            delta,
            visibility(clip_of_group, device, device - offset, count),
        )
        query_total = query_total + query_part
        returned = passed_along(jnp.stack((key_part, value_part)), "ctx", -offset)
        key_total = key_total + returned[0]
        value_total = value_total + returned[1]
    flat = heads_local * HD
    return (
        lax.all_to_all(
            query_total.reshape(rows, flat).astype(jnp.bfloat16),
            "head",
            split_axis=0,
            concat_axis=1,
            tiled=True,
        ),
        lax.all_to_all(
            key_total.reshape(rows, flat).astype(jnp.bfloat16),
            "head",
            split_axis=0,
            concat_axis=1,
            tiled=True,
        ),
        lax.all_to_all(
            value_total.reshape(rows, flat).astype(jnp.bfloat16),
            "head",
            split_axis=0,
            concat_axis=1,
            tiled=True,
        ),
    )


def solution(mesh):
    in_specs = (
        P(("ctx", "head"), None),
        P(("ctx", "head"), None),
        P(("ctx", "head"), None),
        P(("ctx", "head"), None),
        P(("ctx", "head"), None),
        P("head", "ctx"),
        P(),
    )
    out_specs = (P(("ctx", "head"), None), P(("ctx", "head"), None), P(("ctx", "head"), None))
    return jax.shard_map(local, mesh=mesh, in_specs=in_specs, out_specs=out_specs, check_vma=False)
```

profile of v0, /device:TPU:88, one launch (start us, length us, event | category | flops | bytes accessed | tf_op | source)
XLA Modules:
  0.0 461.1 jit_solution(9975940668558790362)
XLA Ops:
  0.6 2.7 copy.86
  3.3 4.3 all-to-all-start.1
  9.2 19.2 %all-to-all-done.1 = bf16[256,4,768]{0,2,1:T(8,128)(2,1)S(1)} async-done(((bf16[256,4,768]{0,2,1:T(8,128)(2,1)}), bf16[256,4,768]{0,2,1:T(8,128)(2,1)S(1)}, u32[]{:S(2)}, u32[]{:S(2)}) %all-to-all-start.1) | async-done | bytes 1572896 | tf_op jit(solution)/shard_map/all_to_all | solution.py:62
  28.3 3.6 all-to-all-start.3
  31.9 2.6 copy.84
  34.5 17.2 %all-to-all-done.3 = bf16[256,4,768]{0,2,1:T(8,128)(2,1)S(1)} async-done(((bf16[256,4,768]{0,2,1:T(8,128)(2,1)}), bf16[256,4,768]{0,2,1:T(8,128)(2,1)S(1)}, u32[]{:S(2)}, u32[]{:S(2)}) %all-to-all-start.3) | async-done | bytes 1572896 | tf_op jit(solution)/shard_map/all_to_all | solution.py:63
  51.7 4.4 all-to-all-start
  60.0 2.6 copy.93
  67.7 3.8 pad_maximum_fusion.2
  76.0 4.7 %all-to-all-start.4 = ((bf16[256,4,768]{0,2,1:T(8,128)(2,1)}), bf16[256,4,768]{0,2,1:T(8,128)(2,1)S(1)}, u32[]{:S(2)}, u32[]{:S(2)}) async-start(bf16[256,4,768]{0,2,1:T(8,128)(2,1)} %bitcast.146), calls=%async_computation.4 | async-start | bytes 3145728 | tf_op jit(solution)/shard_map/all_to_all | solution.py:64
  80.8 2.6 copy.90
  83.3 19.4 %all-to-all-done.4 = bf16[256,4,768]{0,2,1:T(8,128)(2,1)S(1)} async-done(((bf16[256,4,768]{0,2,1:T(8,128)(2,1)}), bf16[256,4,768]{0,2,1:T(8,128)(2,1)S(1)}, u32[]{:S(2)}, u32[]{:S(2)}) %all-to-all-start.4) | async-done | bytes 1572896 | tf_op jit(solution)/shard_map/all_to_all | solution.py:64
  102.7 4.4 all-to-all-start.2
  110.3 3.0 collective-permute-start.1
  113.3 3.8 copy.85
  117.0 3.0 reshape.78
  120.1 3.8 copy.97
  123.8 3.8 reshape.82
  128.4 3.8 copy.91
  132.2 3.8 reshape.80
  138.5 11.5 %fusion.29 = f32[6,1024,1024]{2,1,0:T(8,128)} fusion(bf16[1024,6,128]{0,2,1:T(8,128)(2,1)S(1)} %reshape.78, bf16[2,1024,6,128]{3,1,2,0:T(8,128)(2,1)} %collective-permute-done), kind=kOutput, calls=%fused_computation.42 | convolution fusion | flops 1610612736 | bytes 28311552 | tf_op jit(solution)/shard_map/qhd,khd->hqk/dot_general | solution.py:21
  150.1 15.4 %multiply_convert_fusion.1 = bf16[6,1024,1024]{2,1,0:T(8,128)(2,1)} fusion(f32[6,1024,1024]{2,1,0:T(8,128)} %fusion.29, f32[6,1024]{1,0:T(8,128)S(1)} %fusion.19, f32[6,1024]{1,0:T(8,128)S(1)} %copy-done.9, pred[]{:T(512)} %bitcast.17, bf16[1024,6,128]{0,2,1:T(8,128)(2,1)} %reshape.80, bf16[2,1024,6,128]{3,1,2,0:T(8,128)(2,1)} %collective-permute-done), kind=kOutput, calls=%fused_computation.1 | convolution fusion | flops 1648361472 | bytes 40944128 | tf_op jit(solution)/shard_map/qhd,khd->hqk/dot_general | solution.py:27
  165.4 6.5 %multiply_bitcast_fusion.1 = f32[1,1024,6,128]{3,1,2,0:T(8,128)S(1)} fusion(bf16[6,1024,1024]{2,1,0:T(8,128)(2,1)} %multiply_convert_fusion.1, bf16[1024,6,128]{0,2,1:T(8,128)(2,1)S(1)} %reshape.78), kind=kOutput, calls=%fused_computation.34 | convolution fusion | flops 1611399168 | bytes 17301504 | tf_op jit(solution)/shard_map/hqk,qhd->khd/dot_general | solution.py:33
  172.0 10.7 %fusion.22 = f32[1,1024,6,128]{3,1,2,0:T(8,128)S(1)} fusion(bf16[1024,6,128]{0,2,1:T(8,128)(2,1)S(1)} %copy-done.3, f32[6,1024,1024]{2,1,0:T(8,128)} %fusion.29, f32[6,1024]{1,0:T(8,128)S(1)} %copy-done.9, pred[]{:T(512)} %bitcast.17), kind=kOutput, calls=%fused_computation.35 | convolution fusion | flops 1635778560 | bytes 29908992 | tf_op jit(solution)/shard_map/hqk,qhd->khd/dot_general | solution.py:26
  182.7 3.1 pad_maximum_fusion
  187.7 11.5 %fusion.30 = f32[6,1024,1024]{2,1,0:T(8,128)} fusion(bf16[1024,6,128]{0,2,1:T(8,128)(2,1)S(1)} %reshape.78, bf16[2,1024,6,128]{3,1,2,0:T(8,128)(2,1)} %collective-permute-done.1), kind=kOutput, calls=%fused_computation.43 | convolution fusion | flops 1610612736 | bytes 28311552 | tf_op jit(solution)/shard_map/qhd,khd->hqk/dot_general | solution.py:21
  199.2 11.9 %fusion.25 = f32[1,1024,6,128]{3,1,2,0:T(8,128)} fusion(bf16[1024,6,128]{0,2,1:T(8,128)(2,1)S(1)} %copy-done.3, f32[6,1024,1024]{2,1,0:T(8,128)} %fusion.30, f32[6,1024]{1,0:T(8,128)S(1)} %copy-done.9, pred[]{:T(512)} %bitcast.24), kind=kOutput, calls=%fused_computation.36 | convolution fusion | flops 1635778560 | bytes 29908992 | tf_op jit(solution)/shard_map/hqk,qhd->khd/dot_general | solution.py:26
  211.1 15.3 %multiply_convert_fusion = bf16[6,1024,1024]{2,1,0:T(8,128)(2,1)} fusion(f32[6,1024,1024]{2,1,0:T(8,128)} %fusion.30, f32[6,1024]{1,0:T(8,128)S(1)} %fusion.19, f32[6,1024]{1,0:T(8,128)S(1)} %copy-done.9, pred[]{:T(512)} %bitcast.24, bf16[1024,6,128]{0,2,1:T(8,128)(2,1)} %reshape.80, bf16[2,1024,6,128]{3,1,2,0:T(8,128)(2,1)} %collective-permute-done.1), kind=kOutput, calls=%fused_computation | convolution fusion | flops 1648361472 | bytes 40944128 | tf_op jit(solution)/shard_map/qhd,khd->hqk/dot_general | solution.py:27
  226.4 6.6 %multiply_bitcast_fusion = f32[1,1024,6,128]{3,1,2,0:T(8,128)S(1)} fusion(bf16[6,1024,1024]{2,1,0:T(8,128)(2,1)} %multiply_convert_fusion, bf16[1024,6,128]{0,2,1:T(8,128)(2,1)S(1)} %reshape.78), kind=kOutput, calls=%fused_computation.33 | convolution fusion | flops 1611399168 | bytes 17301504 | tf_op jit(solution)/shard_map/hqk,qhd->khd/dot_general | solution.py:33
  233.0 3.1 pad_maximum_fusion.1
  236.1 2.8 collective-permute-start.3
  241.2 3.9 reshape.81
  245.1 10.1 %fusion.38 = f32[6,1024,1024]{2,1,0:T(8,128)} fusion(bf16[1024,6,128]{0,2,1:T(8,128)(2,1)S(1)} %reshape.78, bf16[1024,6,128]{0,2,1:T(8,128)(2,1)S(1)} %copy-done.1), kind=kOutput, calls=%fused_computation.51 | convolution fusion | flops 1610612736 | bytes 28311552 | tf_op jit(solution)/shard_map/qhd,khd->hqk/dot_general | solution.py:21
  255.3 15.6 %multiply_convert_fusion.2 = bf16[6,1024,1024]{2,1,0:T(8,128)(2,1)} fusion(f32[6,1024,1024]{2,1,0:T(8,128)} %fusion.38, f32[6,1024]{1,0:T(8,128)S(1)} %fusion.19, f32[6,1024]{1,0:T(8,128)S(1)} %copy-done.9, pred[]{:T(512)S(6)} %and.47, bf16[1024,6,128]{0,2,1:T(8,128)(2,1)} %reshape.80, bf16[1024,6,128]{0,2,1:T(8,128)(2,1)} %reshape.81), kind=kOutput, calls=%fused_computation.4 | convolution fusion | flops 1648361472 | bytes 40943616 | tf_op jit(solution)/shard_map/qhd,khd->hqk/dot_general | solution.py:27
  270.8 9.7 %fusion.39 = f32[6,1024,128]{2,1,0:T(8,128)} fusion(bf16[6,1024,1024]{2,1,0:T(8,128)(2,1)} %multiply_convert_fusion.2, bf16[1024,6,128]{0,2,1:T(8,128)(2,1)S(1)} %copy-done.1), kind=kOutput, calls=%fused_computation.52 | convolution fusion | flops 1610612736 | bytes 17301504 | tf_op jit(solution)/shard_map/hqk,khd->qhd/dot_general | solution.py:30
  280.5 10.9 %fusion.28 = f32[6,128,1024]{1,2,0:T(8,128)} fusion(bf16[6,1024,1024]{2,1,0:T(8,128)(2,1)} %multiply_convert_fusion.1, bf16[2,1024,6,128]{3,1,2,0:T(8,128)(2,1)} %collective-permute-done), kind=kOutput, calls=%fused_computation.41 | convolution fusion | flops 1610612736 | bytes 17301504 | tf_op jit(solution)/shard_map/hqk,khd->qhd/dot_general | solution.py:30
  291.4 12.1 %fusion.18 = bf16[1024,6,128]{2,0,1:T(8,128)(2,1)} fusion(f32[6,128,1024]{1,2,0:T(8,128)} %fusion.28, f32[6,1024,128]{2,1,0:T(8,128)} %fusion.39, bf16[6,1024,1024]{2,1,0:T(8,128)(2,1)} %multiply_convert_fusion, bf16[2,1024,6,128]{3,1,2,0:T(8,128)(2,1)} %collective-permute-done.1), kind=kOutput, calls=%fused_computation.29 | convolution fusion | flops 1615331328 | bytes 22020096 | tf_op jit(solution)/shard_map/hqk,khd->qhd/dot_general | solution.py:30
  307.8 2.9 copy.112
  310.7 4.4 all-to-all-start.5
  315.1 79.8 %collective-permute-done.3 = f32[2,1024,6,128]{3,1,2,0:T(8,128)} collective-permute-done((f32[2,1024,6,128]{3,1,2,0:T(8,128)}, f32[2,1024,6,128]{3,1,2,0:T(8,128)}, u32[]{:S(2)}, u32[]{:S(2)}) %collective-permute-start.3) | collective-permute-done | bytes 6291488 | tf_op jit(solution)/shard_map/ppermute | solution.py:15
  394.9 14.5 %fusion.13 = bf16[1024,6,128]{2,0,1:T(8,128)(2,1)} fusion(f32[2,1024,6,128]{3,1,2,0:T(8,128)} %collective-permute-done.3, f32[2,1024,6,128]{3,1,2,0:T(8,128)} %collective-permute-done.2, bf16[1024,6,128]{0,2,1:T(8,128)(2,1)S(1)} %copy-done.4, f32[6,1024,1024]{2,1,0:T(8,128)} %fusion.38, f32[6,1024]{1,0:T(8,128)S(1)} %copy-done.9, pred[]{:T(512)S(6)} %and.47), kind=kOutput, calls=%fused_computation.19 | convolution fusion | flops 1638137856 | bytes 34627584 | tf_op jit(solution)/shard_map/hqk,qhd->khd/dot_general | solution.py:26
  413.5 2.8 copy.124
  416.2 4.4 all-to-all-start.7
  420.7 8.7 %fusion.16 = bf16[1024,6,128]{2,0,1:T(8,128)(2,1)S(1)} fusion(f32[2,1024,6,128]{3,1,2,0:T(8,128)} %collective-permute-done.3, f32[2,1024,6,128]{3,1,2,0:T(8,128)} %collective-permute-done.2, bf16[6,1024,1024]{2,1,0:T(8,128)(2,1)} %multiply_convert_fusion.2, bf16[1024,6,128]{0,2,1:T(8,128)(2,1)S(1)} %reshape.78), kind=kOutput, calls=%fused_computation.24 | convolution fusion | flops 1613758464 | bytes 22020096 | tf_op jit(solution)/shard_map/hqk,qhd->khd/dot_general | solution.py:33
  432.6 9.1 %all-to-all-done.7 = bf16[4,256,768]{1,2,0:T(8,128)(2,1)} async-done(((bf16[4,256,768]{1,2,0:T(8,128)(2,1)}), bf16[4,256,768]{1,2,0:T(8,128)(2,1)}, u32[]{:S(2)}, u32[]{:S(2)}) %all-to-all-start.7) | async-done | bytes 1572896 | tf_op jit(solution)/shard_map/all_to_all | solution.py:121
  441.7 3.6 all-to-all-start.6
  445.3 2.6 copy.125
  450.5 8.5 %all-to-all-done.6 = bf16[4,256,768]{1,2,0:T(8,128)(2,1)S(1)} async-done(((bf16[4,256,768]{1,2,0:T(8,128)(2,1)}), bf16[4,256,768]{1,2,0:T(8,128)(2,1)S(1)}, u32[]{:S(2)}, u32[]{:S(2)}) %all-to-all-start.6) | async-done | bytes 1572896 | tf_op jit(solution)/shard_map/all_to_all | solution.py:114
  (47 shorter events, 39.2 us)
Async XLA Ops:
  0.6 7.0 %copy-start.7 = (bf16[256,3072]{1,0:T(8,128)(2,1)S(1)}, bf16[256,3072]{1,0:T(8,128)(2,1)}, u32[]{:S(2)}) copy-start(bf16[256,3072]{1,0:T(8,128)(2,1)} %param.9) | copy-start | bytes 4718596
  3.3 25.0 %all-to-all-start.1 = ((bf16[256,4,768]{0,2,1:T(8,128)(2,1)}), bf16[256,4,768]{0,2,1:T(8,128)(2,1)S(1)}, u32[]{:S(2)}, u32[]{:S(2)}) async-start(bf16[256,4,768]{0,2,1:T(8,128)(2,1)} %bitcast.4), calls=%async_computation.1 | async-start | bytes 3145728 | tf_op jit(solution)/shard_map/all_to_all | solution.py:62
  28.3 23.3 %all-to-all-start.3 = ((bf16[256,4,768]{0,2,1:T(8,128)(2,1)}), bf16[256,4,768]{0,2,1:T(8,128)(2,1)S(1)}, u32[]{:S(2)}, u32[]{:S(2)}) async-start(bf16[256,4,768]{0,2,1:T(8,128)(2,1)} %bitcast.145), calls=%async_computation.3 | async-start | bytes 3145728 | tf_op jit(solution)/shard_map/all_to_all | solution.py:63
  51.7 4.4 copy-start.5
  51.7 24.3 %all-to-all-start = ((bf16[256,4,768]{0,2,1:T(8,128)(2,1)}), bf16[256,4,768]{0,2,1:T(8,128)(2,1)}, u32[]{:S(2)}, u32[]{:S(2)}) async-start(bf16[256,4,768]{0,2,1:T(8,128)(2,1)} %bitcast.2), calls=%async_computation | async-start | bytes 3145728 | tf_op jit(solution)/shard_map/all_to_all | solution.py:61
  62.7 5.0 %copy-start = (bf16[4,256,768]{1,0,2:T(4,128)(2,1)}, bf16[4,256,768]{1,0,2:T(4,128)(2,1)S(1)}, u32[]{:S(2)}) copy-start(bf16[4,256,768]{1,0,2:T(4,128)(2,1)S(1)} %copy.93) | copy-start | bytes 4718596
  71.5 67.0 %collective-permute-start = (bf16[2,1024,6,128]{3,1,2,0:T(8,128)(2,1)}, bf16[2,1024,6,128]{3,1,2,0:T(8,128)(2,1)}, u32[]{:S(2)}, u32[]{:S(2)}) collective-permute-start(bf16[2,1024,6,128]{3,1,2,0:T(8,128)(2,1)} %pad_maximum_fusion.2), channel_id=1, source_target_pairs={{0,4},{4,8},{8,12},{12,16},{16,20},{20,24},{24,28},{28,32},{32,36}... | collective-permute-start | bytes 9437192 | tf_op jit(solution)/shard_map/ppermute | solution.py:15
  76.0 26.7 %all-to-all-start.4 = ((bf16[256,4,768]{0,2,1:T(8,128)(2,1)}), bf16[256,4,768]{0,2,1:T(8,128)(2,1)S(1)}, u32[]{:S(2)}, u32[]{:S(2)}) async-start(bf16[256,4,768]{0,2,1:T(8,128)(2,1)} %bitcast.146), calls=%async_computation.4 | async-start | bytes 3145728 | tf_op jit(solution)/shard_map/all_to_all | solution.py:64
  80.8 26.4 %copy-start.8 = (s32[32]{0:T(128)S(1)}, s32[32]{0:T(128)}, u32[]{:S(2)}) copy-start(s32[32]{0:T(128)} %param.13) | copy-start | bytes 388
  102.7 10.5 %copy-start.2 = (bf16[256,4,768]{0,2,1:T(8,128)(2,1)}, bf16[256,4,768]{0,2,1:T(8,128)(2,1)S(1)}, u32[]{:S(2)}) copy-start(bf16[256,4,768]{0,2,1:T(8,128)(2,1)S(1)} %all-to-all-done.4) | copy-start | bytes 4718596
  102.7 25.7 %all-to-all-start.2 = ((bf16[256,4,768]{0,2,1:T(8,128)(2,1)}), bf16[256,4,768]{0,2,1:T(8,128)(2,1)}, u32[]{:S(2)}, u32[]{:S(2)}) async-start(bf16[256,4,768]{0,2,1:T(8,128)(2,1)} %bitcast.141), calls=%async_computation.2 | async-start | bytes 3145728 | tf_op jit(solution)/shard_map/all_to_all | solution.py:65
  110.3 77.4 %collective-permute-start.1 = (bf16[2,1024,6,128]{3,1,2,0:T(8,128)(2,1)}, bf16[2,1024,6,128]{3,1,2,0:T(8,128)(2,1)}, u32[]{:S(2)}, u32[]{:S(2)}) collective-permute-start(bf16[2,1024,6,128]{3,1,2,0:T(8,128)(2,1)} %pad_maximum_fusion.2), channel_id=1, source_target_pairs={{0,8},{4,12},{8,16},{12,20},{16,24},{20,28},{24,32},{28,36},{32,40... | collective-permute-start | bytes 9437192 | tf_op jit(solution)/shard_map/ppermute | solution.py:15
  138.5 11.6 %copy-start.9 = (f32[6,1024]{1,0:T(8,128)S(1)}, f32[6,1024]{1,0:T(8,128)}, u32[]{:S(2)}) copy-start(f32[6,1024]{1,0:T(8,128)} %param.12) | copy-start | bytes 73732
  165.4 6.5 %copy-start.3 = (bf16[1024,6,128]{0,2,1:T(8,128)(2,1)S(1)}, bf16[1024,6,128]{0,2,1:T(8,128)(2,1)}, u32[]{:S(2)}) copy-start(bf16[1024,6,128]{0,2,1:T(8,128)(2,1)} %reshape.80) | copy-start | bytes 4718596
  185.7 129.4 %collective-permute-start.2 = (f32[2,1024,6,128]{3,1,2,0:T(8,128)}, f32[2,1024,6,128]{3,1,2,0:T(8,128)}, u32[]{:S(2)}, u32[]{:S(2)}) collective-permute-start(f32[2,1024,6,128]{3,1,2,0:T(8,128)} %pad_maximum_fusion), channel_id=1, source_target_pairs={{4,0},{8,4},{12,8},{16,12},{20,16},{24,20},{28,24},{32,28},{36,32}... | collective-permute-start | bytes 18874376 | tf_op jit(solution)/shard_map/ppermute | solution.py:15
  226.4 6.6 %copy-start.6 = (f32[1,1024,6,128]{3,1,2,0:T(8,128)S(1)}, f32[1,1024,6,128]{3,1,2,0:T(8,128)}, u32[]{:S(2)}) copy-start(f32[1,1024,6,128]{3,1,2,0:T(8,128)} %fusion.25) | copy-start | bytes 9437188
  236.1 158.8 %collective-permute-start.3 = (f32[2,1024,6,128]{3,1,2,0:T(8,128)}, f32[2,1024,6,128]{3,1,2,0:T(8,128)}, u32[]{:S(2)}, u32[]{:S(2)}) collective-permute-start(f32[2,1024,6,128]{3,1,2,0:T(8,128)} %pad_maximum_fusion.1), channel_id=1, source_target_pairs={{8,0},{12,4},{16,8},{20,12},{24,16},{28,20},{32,24},{36,28},{40,32... | collective-permute-start | bytes 18874376 | tf_op jit(solution)/shard_map/ppermute | solution.py:15
  241.2 3.9 copy-start.1
  307.8 87.1 %copy-start.4 = (bf16[1024,6,128]{0,2,1:T(8,128)(2,1)S(1)}, bf16[1024,6,128]{0,2,1:T(8,128)(2,1)}, u32[]{:S(2)}) copy-start(bf16[1024,6,128]{0,2,1:T(8,128)(2,1)} %reshape.80) | copy-start | bytes 4718596
  310.7 105.5 %all-to-all-start.5 = ((bf16[4,256,768]{1,2,0:T(8,128)(2,1)}), bf16[4,256,768]{1,2,0:T(8,128)(2,1)}, u32[]{:S(2)}, u32[]{:S(2)}) async-start(bf16[4,256,768]{1,2,0:T(8,128)(2,1)} %copy.112), calls=%async_computation.5 | async-start | bytes 3145728 | tf_op jit(solution)/shard_map/all_to_all | solution.py:107
  416.2 25.5 %all-to-all-start.7 = ((bf16[4,256,768]{1,2,0:T(8,128)(2,1)}), bf16[4,256,768]{1,2,0:T(8,128)(2,1)}, u32[]{:S(2)}, u32[]{:S(2)}) async-start(bf16[4,256,768]{1,2,0:T(8,128)(2,1)} %copy.124), calls=%async_computation.7 | async-start | bytes 3145728 | tf_op jit(solution)/shard_map/all_to_all | solution.py:121
  441.7 17.2 %all-to-all-start.6 = ((bf16[4,256,768]{1,2,0:T(8,128)(2,1)}), bf16[4,256,768]{1,2,0:T(8,128)(2,1)S(1)}, u32[]{:S(2)}, u32[]{:S(2)}) async-start(bf16[4,256,768]{1,2,0:T(8,128)(2,1)} %copy.120), calls=%async_computation.6 | async-start | bytes 3145728 | tf_op jit(solution)/shard_map/all_to_all | solution.py:114
where the time goes:
time: 468 us; the launch traced here: 461 us
  matrix products  171 us (37%)
  waiting for transfers between devices  154 us (33%)
  local copies, waits for them, and re-layouts  76.5 us (16%)
  starting transfers between devices  43.3 us (9%)
  other arithmetic  12.4 us (3%)
    ppermute x4, waiting for transfers between devices, passed_along(): return lax.ppermute(shard, axis, pairs)  79.8 us
    dot_general x3, matrix products, tile_grads(): jnp.einsum('qhd,khd->hqk', grad_block, value_block, preferred_element_typ...  46.2 us
    dot_general x3, matrix products, tile_grads(): jnp.einsum('hqk,qhd->khd', prob_b, grad_block, preferred_element_type=jnp...  37.1 us
    dot_general x3, matrix products, tile_grads(): jnp.einsum('qhd,khd->hqk', query_block, key_block, preferred_element_type...  33.2 us
    dot_general x3, matrix products, tile_grads(): jnp.einsum('hqk,khd->qhd', dscore, key_block, preferred_element_type=jnp....  32.7 us
    dot_general x3, matrix products, tile_grads(): jnp.einsum('hqk,qhd->khd', dscore, query_block, preferred_element_type=jn...  21.8 us
    all_to_all x1, waiting for transfers between devices, local(): lax.all_to_all(outputs, 'head', split_axis=1, concat_axis=0, tiled=True)  19.4 us
    all_to_all x1, waiting for transfers between devices, local(): lax.all_to_all(keys, 'head', split_axis=1, concat_axis=0, tiled=True)  19.2 us
  transfers between devices with their start and end apart: 12, of which 7 were waited for; matrix products, arithmetic and copies ran while one was open for 55% of the time, Pallas kernels for 0%

commit v1 on v0

v1 whole, which is shorter than its diff:
```python
import functools

import jax
import jax.numpy as jnp
from jax import lax
from jax.experimental import pallas as pl
from jax.experimental.pallas import tpu as pltpu
from jax.sharding import PartitionSpec as P

HD = 128
GROUP = 1024
HEADS = 6
RANKS = 4
COUNT = 32
ROWS = GROUP // RANKS
BQ = 256
MESH = pl.DeviceIdType.MESH
SCALE = HD**-0.5
LOG2E = 1.4426950408889634
HIDDEN = 1e30
f32, bf16 = jnp.float32, jnp.bfloat16


def dot(a, b, ca, cb):
    return lax.dot_general(a, b, (((ca,), (cb,)), ((), ())), preferred_element_type=f32)


def kernel(
    q_in, k_in, v_in, o_in, g_in, lse_in, clip_in,
    q_out, k_out, v_out,
    qg, kv, own, dq, part, relay, back1, back2, stage, o_loc, g_loc, dl_src, dl, lse3,
    in_send, in_recv, kv_send, kv_recv, part_send, relay_recv, back_recv,
    out_send, out_recv, dl_send, dl_recv, loc,
):
    x = lax.axis_index("head")
    c = lax.axis_index("ctx")
    even = lax.rem(c, 2) == 0
    odd = lax.rem(c, 2) == 1

    def rank(p):
        return lax.rem(x + p, RANKS)

    def at_rank(p):
        return {"head": rank(p)}

    def at_ctx(d):
        return {"ctx": lax.rem(c + d + COUNT, COUNT)}

    def arrived(ref, sem):
        pltpu.make_async_copy(ref, ref, sem).wait()

    def remote(src, dst, send, recv, device):
        pltpu.make_async_remote_copy(
            src_ref=src, dst_ref=dst, send_sem=send, recv_sem=recv,
            device_id=device, device_id_type=MESH,
        ).start()

    get_o = pltpu.make_async_copy(o_in, o_loc, loc.at[0])
    get_g = pltpu.make_async_copy(g_in, g_loc, loc.at[1])
    get_o.start()
    get_g.start()

    barrier = pltpu.get_barrier_semaphore()
    for p in range(1, RANKS):
        pl.semaphore_signal(barrier, inc=1, device_id=at_rank(p), device_id_type=MESH)
    for d in (-2, -1, 1, 2):
        pl.semaphore_signal(barrier, inc=1, device_id=at_ctx(d), device_id_type=MESH)
    pl.semaphore_wait(barrier, RANKS - 1 + 4)

    mine = pl.ds(pl.multiple_of(x * ROWS, ROWS), ROWS)

    def fetch(kind, h):
        pair = ((k_in, kv.at[0, h, 0]), (v_in, kv.at[0, h, 1]))
        if kind == 1:
            pair = ((q_in, qg.at[h, 0]), (g_in, qg.at[h, 1]))
        for src, dst in pair:
            for p in (1, 3, 2, 0):
                cols = pl.ds(pl.multiple_of((rank(p) * HEADS + h) * HD, HD), HD)
                if p == 0:
                    pltpu.make_async_copy(src.at[:, cols], dst.at[mine], in_recv.at[kind, h]).start()
                else:
                    remote(src.at[:, cols], dst.at[mine], in_send.at[kind, h], in_recv.at[kind, h], at_rank(p))

    def fetch_head(h, _):
        fetch(0, h)
        fetch(1, h)
        return 0

    lax.fori_loop(0, HEADS, fetch_head, 0)

    get_o.wait()
    get_g.wait()
    lane = lax.broadcasted_iota(jnp.int32, (ROWS, HD), 1)
    delta = jnp.zeros((ROWS, HD), f32)
    for r in range(RANKS):
        for h in range(HEADS):
            cols = pl.ds((r * HEADS + h) * HD, HD)
            prod = o_loc[:, cols].astype(f32) * g_loc[:, cols].astype(f32)
            total = jnp.sum(prod, axis=1, keepdims=True)
            delta = jnp.where(lane == r * 8 + h, total, delta)
    flipped = delta.T
    for r in range(RANKS):
        dl_src[r] = flipped[r * 8 : (r + 1) * 8]
    for p in range(RANKS):
        if p == 0:
            pltpu.make_async_copy(dl_src.at[x], dl.at[:, mine], dl_recv).start()
        else:
            remote(dl_src.at[rank(p)], dl.at[:, mine], dl_send, dl_recv, at_rank(p))

    here = clip_in[c]
    lse = lse_in[...] * LOG2E
    lse3[0] = lse
    for j in (1, 2):
        seen = jnp.logical_and(clip_in[lax.max(c - j, 0)] == here, c >= j)
        lse3[j] = jnp.where(seen, lse, HIDDEN)
    arrived(dl, dl_recv)

    def give(h):
        arrived(kv.at[0, h], in_recv.at[0, h])
        remote(kv.at[0, h], kv.at[1, h], kv_send.at[0, h], kv_recv.at[0, h], at_ctx(1))

        @pl.when(even)
        def _():
            remote(kv.at[0, h], kv.at[2, h], kv_send.at[1, h], kv_recv.at[1, h], at_ctx(2))

    def grads(h, j):
        key = kv[j, h, 0]
        value = kv[j, h, 1]
        dk = jnp.zeros((GROUP, HD), f32)
        dv = jnp.zeros((GROUP, HD), f32)
        for t in range(GROUP // BQ):
            rows = pl.ds(t * BQ, BQ)
            query = qg[h, 0, rows]
            grad = qg[h, 1, rows]
            score = dot(key, query, 1, 1)
            prob = jnp.exp2(score * (SCALE * LOG2E) - lse3[j, pl.ds(h, 1), rows])
            dprob = dot(value, grad, 1, 1)
            dscore = (prob * (dprob - dl[pl.ds(h, 1), rows])).astype(bf16)
            dv += dot(prob.astype(bf16), grad, 1, 0)
            dk += dot(dscore, query, 1, 0)
            step = dot(dscore, key, 0, 0)
            if j == 0:
                dq[h, rows] = step
            elif j == 1:
                dq[h, rows] += step
            else:
                stage[0, h, rows] = ((dq[h, rows] + step) * SCALE).astype(bf16)
        if j == 0:
            own[h, 0] = dk
            own[h, 1] = dv
        else:
            part[j - 1, h, 0] = dk.astype(bf16)
            part[j - 1, h, 1] = dv.astype(bf16)

    def put(which, out, h):
        cols = pl.ds(pl.multiple_of((x * HEADS + h) * HD, HD), HD)
        for p in (1, 3, 2, 0):
            src = stage.at[which, h, pl.ds(pl.multiple_of(rank(p) * ROWS, ROWS), ROWS)]
            if p == 0:
                pltpu.make_async_copy(src, out.at[:, cols], out_recv.at[which]).start()
            else:
                remote(src, out.at[:, cols], out_send.at[which, h], out_recv.at[which], at_rank(p))

    give(0)

    def step(i, _):
        @pl.when(i < HEADS)
        def _():
            arrived(qg.at[i], in_recv.at[1, i])
            grads(i, 0)

        @pl.when(i + 1 < HEADS)
        def _():
            give(i + 1)

        inner = jnp.logical_and(i >= 1, i <= HEADS)

        @pl.when(inner)
        def _():
            h = i - 1
            arrived(kv.at[1, h], kv_recv.at[0, h])

            @pl.when(even)
            def _():
                remote(kv.at[1, h], kv.at[2, h], kv_send.at[2, h], kv_recv.at[1, h], at_ctx(1))

            grads(h, 1)

            @pl.when(odd)
            def _():
                remote(part.at[0, h], back1.at[h], part_send.at[0, h], back_recv.at[0, h], at_ctx(-1))

            arrived(kv.at[2, h], kv_recv.at[1, h])
            grads(h, 2)

            @pl.when(odd)
            def _():
                remote(part.at[1, h], relay.at[h], part_send.at[1, h], relay_recv.at[h], at_ctx(-1))

            @pl.when(even)
            def _():
                remote(part.at[1, h], back2.at[h], part_send.at[1, h], back_recv.at[1, h], at_ctx(-2))

            put(0, q_out, h)

        @pl.when(i >= 2)
        def _():
            h = i - 2
            arrived(back1.at[h], back_recv.at[0, h])

            @pl.when(even)
            def _():
                arrived(back2.at[h], back_recv.at[1, h])
                dk = own[h, 0] + back1[h, 0].astype(f32) + back2[h, 0].astype(f32)
                dv = own[h, 1] + back1[h, 1].astype(f32) + back2[h, 1].astype(f32)
                stage[1, h] = (dk * SCALE).astype(bf16)
                stage[2, h] = dv.astype(bf16)

            @pl.when(odd)
            def _():
                stage[1, h] = ((own[h, 0] + back1[h, 0].astype(f32)) * SCALE).astype(bf16)
                stage[2, h] = (own[h, 1] + back1[h, 1].astype(f32)).astype(bf16)

            put(1, k_out, h)
            put(2, v_out, h)

        @pl.when(jnp.logical_and(inner, even))
        def _():
            h = i - 1
            arrived(relay.at[h], relay_recv.at[h])
            for n in range(2):
                part[0, h, n] = (part[0, h, n].astype(f32) + relay[h, n].astype(f32)).astype(bf16)
            remote(part.at[0, h], back1.at[h], part_send.at[0, h], back_recv.at[0, h], at_ctx(-1))

        return 0

    lax.fori_loop(0, HEADS + 2, step, 0)

    most = pl.ds(0, GROUP - ROWS)
    for r in range(1, RANKS):
        arrived(dl_src.at[r], dl_send)

    def drain(h, _):
        arrived(kv.at[0, h, :, most], in_send.at[0, h])
        arrived(qg.at[h, :, most], in_send.at[1, h])
        arrived(kv.at[0, h], kv_send.at[0, h])
        arrived(part.at[0, h], part_send.at[0, h])
        arrived(part.at[1, h], part_send.at[1, h])
        for n in range(3):
            arrived(stage.at[n, h, most], out_send.at[n, h])

        @pl.when(even)
        def _():
            arrived(kv.at[0, h], kv_send.at[1, h])
            arrived(kv.at[1, h], kv_send.at[2, h])

        return 0

    lax.fori_loop(0, HEADS, drain, 0)
    arrived(q_out, out_recv.at[0])
    arrived(k_out, out_recv.at[1])
    arrived(v_out, out_recv.at[2])


def local(queries, keys, values, outputs, out_grad, logsumexp, clip_of_group):
    hbm = pl.BlockSpec(memory_space=pl.ANY)
    vmem = pl.BlockSpec(memory_space=pltpu.VMEM)
    smem = pl.BlockSpec(memory_space=pltpu.SMEM)
    dma = pltpu.SemaphoreType.DMA
    whole = (2, GROUP, HD)
    out = jax.ShapeDtypeStruct((ROWS, RANKS * HEADS * HD), bf16)
    return pl.pallas_call(
        kernel,
        out_shape=(out, out, out),
        in_specs=[hbm, hbm, hbm, hbm, hbm, vmem, smem],
        out_specs=(hbm, hbm, hbm),
        scratch_shapes=[
            pltpu.VMEM((HEADS, *whole), bf16),
            pltpu.VMEM((3, HEADS, *whole), bf16),
            pltpu.VMEM((HEADS, *whole), f32),
            pltpu.VMEM((HEADS, GROUP, HD), f32),
            pltpu.VMEM((2, HEADS, *whole), bf16),
            pltpu.VMEM((HEADS, *whole), bf16),
            pltpu.VMEM((HEADS, *whole), bf16),
            pltpu.VMEM((HEADS, *whole), bf16),
            pltpu.VMEM((3, HEADS, GROUP, HD), bf16),
            pltpu.VMEM((ROWS, RANKS * HEADS * HD), bf16),
            pltpu.VMEM((ROWS, RANKS * HEADS * HD), bf16),
            pltpu.VMEM((RANKS, 8, ROWS), f32),
            pltpu.VMEM((8, GROUP), f32),
            pltpu.VMEM((3, HEADS, GROUP), f32),
            dma((2, HEADS)),
            dma((2, HEADS)),
            dma((3, HEADS)),
            dma((2, HEADS)),
            dma((2, HEADS)),
            dma((HEADS,)),
            dma((2, HEADS)),
            dma((3, HEADS)),
            dma((3,)),
            dma,
            dma,
            dma((2,)),
        ],
        cost_estimate=pl.CostEstimate(
            flops=2 * 5 * 3 * HEADS * GROUP * GROUP * HD,
            bytes_accessed=12 * 2**20,
            transcendentals=3 * HEADS * GROUP * GROUP,
        ),
        compiler_params=pltpu.CompilerParams(
            collective_id=0, has_side_effects=True, vmem_limit_bytes=58 * 2**20
        ),
        name="clip_attention_backward",
    )(queries, keys, values, outputs, out_grad, logsumexp, clip_of_group)


def solution(mesh):
    rows = P(("ctx", "head"), None)
    return jax.shard_map(
        local,
        mesh=mesh,
        in_specs=(rows, rows, rows, rows, rows, P("head", "ctx"), P()),
        out_specs=(rows, rows, rows),
        check_vma=False,
    )
```

time: 468 us -> 179 us (0.38)
  the two profiles are of different devices: /device:TPU:88 before, /device:TPU:1 now
where the time goes in v1:
time: 179 us
  Pallas kernels  173 us (97%)
  local copies, waits for them, and re-layouts  5.89 us (3%)
    pallas_call x1, Pallas kernels, local(): pl.pallas_call(kernel, out_shape=(out, out, out), in_specs=[hbm, hbm, hbm...  173 us
    unnamed x7, local copies, waits for them, and re-layouts  5.89 us

profile of v1, /device:TPU:1, one launch (start us, length us, event | category | flops | bytes accessed | tf_op | source)
XLA Modules:
  0.0 179.2 jit_solution(15768313197320583337)
XLA Ops:
  0.6 172.6 %clip_attention_backward.1 = (bf16[256,3072]{1,0:T(8,128)(2,1)}, bf16[256,3072]{1,0:T(8,128)(2,1)}, bf16[256,3072]{1,0:T(8,128)(2,1)}) custom-call(bf16[256,3072]{1,0:T(8,128)(2,1)} %q_in.1, bf16[256,3072]{1,0:T(8,128)(2,1)} %k_in.1, bf16[256,3072]{1,0:T(8,128)(2,1)} %v_in.1, bf16[256,3072]{1,0:T(8,128)(2,1)} %o_in.1, bf16[256,3072]{1,0:T(8,128)(2,1)} %g_in.1, ...), custom_call_target="tpu_custom_call" | custom-call | flops 24159191040 | bytes 12582912 | tf_op jit(solution)/shard_map/clip_attention_backward/pallas_call | solution.py:272
  173.3 0.0 copy-start.1
  173.3 2.8 %copy.13 = bf16[256,3072]{1,0:T(8,128)(2,1)} copy(bf16[256,3072]{1,0:T(8,128)(2,1)} %get-tuple-element.6) | data formatting | bytes 3145728
  176.0 0.0 copy-done.1
  176.1 0.0 copy-start
  176.1 1.1 copy.14
  177.2 0.8 copy-done
  178.0 1.1 copy.15
Async XLA Ops:
  173.3 2.8 %copy-start.1 = (bf16[256,3072]{1,0:T(8,128)(2,1)S(1)}, bf16[256,3072]{1,0:T(8,128)(2,1)}, u32[]{:S(2)}) copy-start(bf16[256,3072]{1,0:T(8,128)(2,1)} %get-tuple-element.7) | copy-start | bytes 4718596
  176.1 2.0 %copy-start = (bf16[256,3072]{1,0:T(8,128)(2,1)S(1)}, bf16[256,3072]{1,0:T(8,128)(2,1)}, u32[]{:S(2)}) copy-start(bf16[256,3072]{1,0:T(8,128)(2,1)} %get-tuple-element.8) | copy-start | bytes 4718596

commit v2 on v1

--- a/solution.py
+++ b/solution.py
@@ -81,12 +81,10 @@
                 else:
                     remote(src.at[:, cols], dst.at[mine], in_send.at[kind, h], in_recv.at[kind, h], at_rank(p))
 
-    def fetch_head(h, _):
-        fetch(0, h)
-        fetch(1, h)
-        return 0
-
-    lax.fori_loop(0, HEADS, fetch_head, 0)
+    fetch(0, 0)
+    fetch(1, 0)
+    fetch(0, 1)
+    fetch(1, 1)
 
     get_o.wait()
     get_g.wait()
@@ -167,11 +165,22 @@
         @pl.when(i < HEADS)
         def _():
             arrived(qg.at[i], in_recv.at[1, i])
+
+        @pl.when(i + 2 < HEADS)
+        def _():
+            fetch(0, i + 2)
+
+        @pl.when(i < HEADS)
+        def _():
             grads(i, 0)
 
         @pl.when(i + 1 < HEADS)
         def _():
             give(i + 1)
+
+        @pl.when(i + 2 < HEADS)
+        def _():
+            fetch(1, i + 2)
 
         inner = jnp.logical_and(i >= 1, i <= HEADS)
 

time: 179 us -> 141 us (0.79)
  Pallas kernels: 173 us -> 134 us
    pallas_call x1, Pallas kernels: 173 us -> 134 us  [local(): pl.pallas_call(kernel, out_shape=(out, out, out), in_specs=[hbm, hbm, hbm...]
where the time goes in v2:
time: 141 us
  Pallas kernels  134 us (95%)
  local copies, waits for them, and re-layouts  5.89 us (4%)
    pallas_call x1, Pallas kernels, local(): pl.pallas_call(kernel, out_shape=(out, out, out), in_specs=[hbm, hbm, hbm...  134 us
    unnamed x7, local copies, waits for them, and re-layouts  5.89 us

profile of v2, /device:TPU:1, one launch (start us, length us, event | category | flops | bytes accessed | tf_op | source)
XLA Modules:
  0.0 140.8 jit_solution(9450111562268463484)
XLA Ops:
  0.6 134.2 %clip_attention_backward.1 = (bf16[256,3072]{1,0:T(8,128)(2,1)}, bf16[256,3072]{1,0:T(8,128)(2,1)}, bf16[256,3072]{1,0:T(8,128)(2,1)}) custom-call(bf16[256,3072]{1,0:T(8,128)(2,1)} %q_in.1, bf16[256,3072]{1,0:T(8,128)(2,1)} %k_in.1, bf16[256,3072]{1,0:T(8,128)(2,1)} %v_in.1, bf16[256,3072]{1,0:T(8,128)(2,1)} %o_in.1, bf16[256,3072]{1,0:T(8,128)(2,1)} %g_in.1, ...), custom_call_target="tpu_custom_call" | custom-call | flops 24159191040 | bytes 12582912 | tf_op jit(solution)/shard_map/clip_attention_backward/pallas_call | solution.py:281
  134.9 0.0 copy-start.1
  134.9 2.8 %copy.13 = bf16[256,3072]{1,0:T(8,128)(2,1)} copy(bf16[256,3072]{1,0:T(8,128)(2,1)} %get-tuple-element.6) | data formatting | bytes 3145728
  137.6 0.0 copy-done.1
  137.6 0.0 copy-start
  137.6 1.1 copy.14
  138.8 0.8 copy-done
  139.6 1.1 copy.15
Async XLA Ops:
  134.9 2.8 %copy-start.1 = (bf16[256,3072]{1,0:T(8,128)(2,1)S(1)}, bf16[256,3072]{1,0:T(8,128)(2,1)}, u32[]{:S(2)}) copy-start(bf16[256,3072]{1,0:T(8,128)(2,1)} %get-tuple-element.7) | copy-start | bytes 4718596
  137.6 2.0 %copy-start = (bf16[256,3072]{1,0:T(8,128)(2,1)S(1)}, bf16[256,3072]{1,0:T(8,128)(2,1)}, u32[]{:S(2)}) copy-start(bf16[256,3072]{1,0:T(8,128)(2,1)} %get-tuple-element.8) | copy-start | bytes 4718596

commit v3 on v1

v3 whole, which is shorter than its diff:
```python
import jax
import jax.numpy as jnp
from jax import lax
from jax.experimental import pallas as pl
from jax.experimental.pallas import tpu as pltpu
from jax.sharding import PartitionSpec as P

HD = 128
GROUP = 1024
HEADS = 6
RANKS = 4
COUNT = 32
ROWS = GROUP // RANKS
KEYS = 2 * ROWS
BQ = 1024
AHEAD = 2
HOLD = 5
HOLD_DQ = 4
MESH = pl.DeviceIdType.MESH
SCALE = HD**-0.5
LOG2E = 1.4426950408889634
HIDDEN = 1e30
f32, bf16 = jnp.float32, jnp.bfloat16


def dot(a, b, ca, cb):
    return lax.dot_general(a, b, (((ca,), (cb,)), ((), ())), preferred_element_type=f32)


def kernel(
    q_in, k_in, v_in, o_in, g_in, lse_in, clip_in,
    q_out, k_out, v_out,
    qg, kv, own, dq, dq_away, dq_in, part, relay, back1, back2, stage, o_loc, g_loc, dl_src, dl, lse_far, lse3,
    in_send, kv_in, outer_in, q_in_sem, fwd_send, kv_send, kv_recv, part_send, relay_recv, back_recv,
    dq_send, dq_recv, out_send, out_recv, dl_send, dl_recv, loc,
):
    x = lax.axis_index("head")
    c = lax.axis_index("ctx")
    even = lax.rem(c, 2) == 0
    odd = lax.rem(c, 2) == 1

    def rank(p):
        return lax.rem(x + p + RANKS, RANKS)

    def at_rank(p):
        return {"head": rank(p)}

    def at_ctx(d):
        return {"ctx": lax.rem(c + d + COUNT, COUNT)}

    def arrived(ref, sem):
        pltpu.make_async_copy(ref, ref, sem).wait()

    def remote(src, dst, send, recv, device):
        pltpu.make_async_remote_copy(
            src_ref=src, dst_ref=dst, send_sem=send, recv_sem=recv,
            device_id=device, device_id_type=MESH,
        ).start()

    def block(p):
        return pl.ds(pl.multiple_of(rank(p) * ROWS, ROWS), ROWS)

    def head_cols(p, h):
        return pl.ds(pl.multiple_of((rank(p) * HEADS + h) * HD, HD), HD)

    SIDE = (1, -1)
    SET = (0, -1)
    NEAR, FAR = pl.ds(0, ROWS), pl.ds(ROWS, ROWS)

    get_o = pltpu.make_async_copy(o_in, o_loc, loc.at[0])
    get_g = pltpu.make_async_copy(g_in, g_loc, loc.at[1])
    get_o.start()
    get_g.start()

    barrier = pltpu.get_barrier_semaphore()
    for p in range(1, RANKS):
        pl.semaphore_signal(barrier, inc=1, device_id=at_rank(p), device_id_type=MESH)
    for d in (-2, -1, 1, 2):
        pl.semaphore_signal(barrier, inc=1, device_id=at_ctx(d), device_id_type=MESH)
    pl.semaphore_wait(barrier, RANKS - 1 + 4)

    def fetch_outer(h):
        for role in (0, 1):
            side = SIDE[role]
            cols = head_cols(side + SET[role], h)
            for n, src in ((0, q_in), (1, g_in)):
                remote(src.at[:, cols], qg.at[h, role, n, block(0)], in_send.at[h], outer_in.at[h], at_rank(side))
        for role in (0, 1):
            side = SIDE[role]
            cols = head_cols(side + SET[role], h)
            for n, src in ((0, k_in), (1, v_in)):
                remote(src.at[:, cols], kv.at[0, h, role, n, FAR], in_send.at[h], kv_in.at[h], at_rank(side))
        for role in (0, 1):
            cols = head_cols(SET[role], h)
            for n, src in ((0, k_in), (1, v_in)):
                pltpu.make_async_copy(src.at[:, cols], kv.at[0, h, role, n, NEAR], kv_in.at[h]).start()

    def fetch_own(h):
        for role in (0, 1):
            cols = head_cols(SET[role], h)
            for n, src in ((0, q_in), (1, g_in)):
                remote(
                    src.at[:, cols], qg.at[h, 1 - role, n, block(0)],
                    in_send.at[h], q_in_sem.at[h], at_rank(SIDE[role]),
                )
                pltpu.make_async_copy(src.at[:, cols], qg.at[h, role, n, block(0)], q_in_sem.at[h]).start()

    def forward(h):
        arrived(qg.at[h, :, :, NEAR], outer_in.at[h])
        for role in (0, 1):
            outer = block(-SIDE[role])
            remote(
                qg.at[h, role, :, outer], qg.at[h, 1 - role, :, outer],
                fwd_send.at[h], q_in_sem.at[h], at_rank(SIDE[role]),
            )

    def give(h):
        arrived(kv.at[0, h], kv_in.at[h])
        remote(kv.at[0, h], kv.at[1, h], kv_send.at[0, h], kv_recv.at[0, h], at_ctx(1))

        @pl.when(even)
        def _():
            remote(kv.at[0, h], kv.at[2, h], kv_send.at[1, h], kv_recv.at[1, h], at_ctx(2))

    for h in range(AHEAD):
        fetch_outer(h)
        fetch_own(h)
    remote(lse_in, lse_far, dl_send.at[0], dl_recv.at[0], at_rank(1))

    get_o.wait()
    get_g.wait()
    lane = lax.broadcasted_iota(jnp.int32, (ROWS, HD), 1)
    delta = jnp.zeros((ROWS, HD), f32)
    for r in range(RANKS):
        for h in range(HEADS):
            cols = pl.ds((r * HEADS + h) * HD, HD)
            prod = o_loc[:, cols].astype(f32) * g_loc[:, cols].astype(f32)
            total = jnp.sum(prod, axis=1, keepdims=True)
            delta = jnp.where(lane == r * 8 + h, total, delta)
    flipped = delta.T
    for r in range(RANKS):
        dl_src[r] = flipped[r * 8 : (r + 1) * 8]
    for role in (0, 1):
        for p in range(RANKS):
            src, dst = dl_src.at[rank(p + SET[role])], dl.at[role, :, block(0)]
            if p == 0:
                pltpu.make_async_copy(src, dst, dl_recv.at[1]).start()
            else:
                remote(src, dst, dl_send.at[1], dl_recv.at[1], at_rank(p))

    give(0)
    forward(0)

    arrived(lse_far, dl_recv.at[0])
    here = clip_in[c]
    for role, src in ((0, lse_in), (1, lse_far)):
        lse = src[...] * LOG2E
        lse3[role, 0] = lse
        for j in (1, 2):
            seen = jnp.logical_and(clip_in[lax.max(c - j, 0)] == here, c >= j)
            lse3[role, j] = jnp.where(seen, lse, HIDDEN)
    arrived(dl, dl_recv.at[1])

    def grads(h, j):
        def one(role, _):
            key = kv[j, h, role, 0]
            value = kv[j, h, role, 1]
            dk = jnp.zeros((KEYS, HD), f32)
            dv = jnp.zeros((KEYS, HD), f32)
            for t in range(GROUP // BQ):
                rows = pl.ds(t * BQ, BQ)
                query = qg[h, role, 0, rows]
                grad = qg[h, role, 1, rows]
                score = dot(key, query, 1, 1)
                prob = jnp.exp2(score * (SCALE * LOG2E) - lse3[role, j, pl.ds(h, 1), rows])
                dprob = dot(value, grad, 1, 1)
                dscore = (prob * (dprob - dl[role, pl.ds(h, 1), rows])).astype(bf16)
                dv += dot(prob.astype(bf16), grad, 1, 0)
                dk += dot(dscore, query, 1, 0)
                step = dot(key, dscore, 0, 0)
                if j == 0:
                    dq[h, role, :, rows] = step
                else:
                    dq[h, role, :, rows] += step
            if j == 0:
                own[h, role, 0] = dk
                own[h, role, 1] = dv
            else:
                part[j - 1, h, role, 0] = dk.astype(bf16)
                part[j - 1, h, role, 1] = dv.astype(bf16)
            return 0

        lax.fori_loop(0, 2, one, 0)

    def put(which, out, h):
        for role in (0, 1):
            cols = head_cols(SET[role], h)
            remote(
                stage.at[which, h, role, FAR], out.at[:, cols],
                out_send.at[which, h], out_recv.at[which], at_rank(-SIDE[role]),
            )
            pltpu.make_async_copy(stage.at[which, h, role, NEAR], out.at[:, cols], out_recv.at[which]).start()

    def share_dq(h):
        for role in (0, 1):
            dq_away[h, role, NEAR] = dq[h, role, :, block(SIDE[role])].T.astype(bf16)
            dq_away[h, role, FAR] = dq[h, role, :, block(2)].T.astype(bf16)
            remote(dq_away.at[h, role], dq_in.at[h, 1 - role], dq_send.at[h], dq_recv.at[h], at_rank(SIDE[role]))

    def finish_dq(h):
        arrived(dq_in.at[h], dq_recv.at[h])
        for role in (0, 1):
            for where, p in ((NEAR, 0), (FAR, -SIDE[role])):
                total = dq[h, role, :, block(p)].T + dq_in[h, role, where].astype(f32)
                stage[0, h, role, where] = (total * SCALE).astype(bf16)
        put(0, q_out, h)

    def finish_kv(h):
        arrived(back1.at[h], back_recv.at[0, h])

        @pl.when(even)
        def _():
            arrived(back2.at[h], back_recv.at[1, h])
            for n, factor in ((0, SCALE), (1, 1.0)):
                for role in (0, 1):
                    total = own[h, role, n] + back1[h, role, n].astype(f32) + back2[h, role, n].astype(f32)
                    stage[1 + n, h, role] = (total * factor).astype(bf16)

        @pl.when(odd)
        def _():
            for n, factor in ((0, SCALE), (1, 1.0)):
                for role in (0, 1):
                    total = own[h, role, n] + back1[h, role, n].astype(f32)
                    stage[1 + n, h, role] = (total * factor).astype(bf16)

    def put_kv(h):
        put(1, k_out, h)
        put(2, v_out, h)

    def later(i, first, lag, do):
        @pl.when(i == first)
        def _():
            def each(h, _):
                do(h)
                return 0

            lax.fori_loop(0, first - lag + 1, each, 0)

        @pl.when(jnp.logical_and(i > first, i - lag < HEADS))
        def _():
            do(i - lag)

    def step(i, _):
        @pl.when(i + AHEAD < HEADS)
        def _():
            fetch_outer(i + AHEAD)

        @pl.when(i < HEADS)
        def _():
            arrived(qg.at[i, :, :, pl.ds(0, GROUP - ROWS)], q_in_sem.at[i])
            grads(i, 0)

        @pl.when(i + 1 < HEADS)
        def _():
            give(i + 1)
            forward(i + 1)

        @pl.when(i + AHEAD < HEADS)
        def _():
            fetch_own(i + AHEAD)

        inner = jnp.logical_and(i >= 1, i <= HEADS)

        @pl.when(inner)
        def _():
            h = i - 1
            arrived(kv.at[1, h], kv_recv.at[0, h])

            @pl.when(even)
            def _():
                remote(kv.at[1, h], kv.at[2, h], kv_send.at[2, h], kv_recv.at[1, h], at_ctx(1))

            grads(h, 1)

            @pl.when(odd)
            def _():
                remote(part.at[0, h], back1.at[h], part_send.at[0, h], back_recv.at[0, h], at_ctx(-1))

            arrived(kv.at[2, h], kv_recv.at[1, h])
            grads(h, 2)

            @pl.when(odd)
            def _():
                remote(part.at[1, h], relay.at[h], part_send.at[1, h], relay_recv.at[h], at_ctx(-1))

            @pl.when(even)
            def _():
                remote(part.at[1, h], back2.at[h], part_send.at[1, h], back_recv.at[1, h], at_ctx(-2))

        later(i, HOLD_DQ, 1, share_dq)

        @pl.when(i >= 2)
        def _():
            finish_kv(i - 2)

        later(i, HOLD, 2, put_kv)
        later(i, HOLD, 2, finish_dq)

        @pl.when(jnp.logical_and(inner, even))
        def _():
            h = i - 1
            arrived(relay.at[h], relay_recv.at[h])
            for role in (0, 1):
                for n in (0, 1):
                    total = part[0, h, role, n].astype(f32) + relay[h, role, n].astype(f32)
                    part[0, h, role, n] = total.astype(bf16)
            remote(part.at[0, h], back1.at[h], part_send.at[0, h], back_recv.at[0, h], at_ctx(-1))

        return 0

    lax.fori_loop(0, HEADS + 2, step, 0)

    arrived(lse_in, dl_send.at[0])
    for r in range(1, RANKS):
        arrived(dl_src.at[pl.ds(0, 2)], dl_send.at[1])

    def drain(h, _):
        arrived(qg.at[h, :, :, pl.ds(0, GROUP - ROWS)], in_send.at[h])
        arrived(qg.at[h, :, :, NEAR], fwd_send.at[h])
        arrived(kv.at[0, h], kv_send.at[0, h])
        arrived(part.at[0, h], part_send.at[0, h])
        arrived(part.at[1, h], part_send.at[1, h])
        arrived(dq_away.at[h], dq_send.at[h])
        for n in range(3):
            arrived(stage.at[n, h, :, NEAR], out_send.at[n, h])

        @pl.when(even)
        def _():
            arrived(kv.at[0, h], kv_send.at[1, h])
            arrived(kv.at[1, h], kv_send.at[2, h])

        return 0

    lax.fori_loop(0, HEADS, drain, 0)
    arrived(q_out, out_recv.at[0])
    arrived(k_out, out_recv.at[1])
    arrived(v_out, out_recv.at[2])


def local(queries, keys, values, outputs, out_grad, logsumexp, clip_of_group):
    hbm = pl.BlockSpec(memory_space=pl.ANY)
    vmem = pl.BlockSpec(memory_space=pltpu.VMEM)
    smem = pl.BlockSpec(memory_space=pltpu.SMEM)
    dma = pltpu.SemaphoreType.DMA
    half = (HEADS, 2, 2, KEYS, HD)
    out = jax.ShapeDtypeStruct((ROWS, RANKS * HEADS * HD), bf16)
    return pl.pallas_call(
        kernel,
        out_shape=(out, out, out),
        in_specs=[hbm, hbm, hbm, hbm, hbm, vmem, smem],
        out_specs=(hbm, hbm, hbm),
        scratch_shapes=[
            pltpu.VMEM((HEADS, 2, 2, GROUP, HD), bf16),
            pltpu.VMEM((3, *half), bf16),
            pltpu.VMEM(half, f32),
            pltpu.VMEM((HEADS, 2, HD, GROUP), f32),
            pltpu.VMEM((HEADS, 2, KEYS, HD), bf16),
            pltpu.VMEM((HEADS, 2, KEYS, HD), bf16),
            pltpu.VMEM((2, *half), bf16),
            pltpu.VMEM(half, bf16),
            pltpu.VMEM(half, bf16),
            pltpu.VMEM(half, bf16),
            pltpu.VMEM((3, HEADS, 2, KEYS, HD), bf16),
            pltpu.VMEM((ROWS, RANKS * HEADS * HD), bf16),
            pltpu.VMEM((ROWS, RANKS * HEADS * HD), bf16),
            pltpu.VMEM((RANKS, 8, ROWS), f32),
            pltpu.VMEM((2, 8, GROUP), f32),
            pltpu.VMEM((HEADS, GROUP), f32),
            pltpu.VMEM((2, 3, HEADS, GROUP), f32),
            dma((HEADS,)),
            dma((HEADS,)),
            dma((HEADS,)),
            dma((HEADS,)),
            dma((HEADS,)),
            dma((3, HEADS)),
            dma((2, HEADS)),
            dma((2, HEADS)),
            dma((HEADS,)),
            dma((2, HEADS)),
            dma((HEADS,)),
            dma((HEADS,)),
            dma((3, HEADS)),
            dma((3,)),
            dma((2,)),
            dma((2,)),
            dma((2,)),
        ],
        cost_estimate=pl.CostEstimate(
            flops=2 * 5 * 3 * HEADS * GROUP * GROUP * HD,
            bytes_accessed=12 * 2**20,
            transcendentals=3 * HEADS * GROUP * GROUP,
        ),
        compiler_params=pltpu.CompilerParams(
            collective_id=0, has_side_effects=True, vmem_limit_bytes=60 * 2**20
        ),
        name="clip_attention_backward",
    )(queries, keys, values, outputs, out_grad, logsumexp, clip_of_group)


def solution(mesh):
    rows = P(("ctx", "head"), None)
    return jax.shard_map(
        local,
        mesh=mesh,
        in_specs=(rows, rows, rows, rows, rows, P("head", "ctx"), P()),
        out_specs=(rows, rows, rows),
        check_vma=False,
    )
```

time: 179 us -> 136 us (0.76)
  Pallas kernels: 173 us -> 129 us
    pallas_call x1, Pallas kernels: 173 us -> 129 us  [local(): pl.pallas_call(kernel, out_shape=(out, out, out), in_specs=[hbm, hbm, hbm...]
where the time goes in v3:
time: 136 us; the launch traced here: 135 us
  Pallas kernels  129 us (95%)
  local copies, waits for them, and re-layouts  5.89 us (4%)
    pallas_call x1, Pallas kernels, local(): pl.pallas_call(kernel, out_shape=(out, out, out), in_specs=[hbm, hbm, hbm...  129 us
    unnamed x7, local copies, waits for them, and re-layouts  5.89 us

profile of v3, /device:TPU:1, one launch (start us, length us, event | category | flops | bytes accessed | tf_op | source)
XLA Modules:
  0.0 135.3 jit_solution(16919941877265812934)
XLA Ops:
  0.6 128.8 %clip_attention_backward.1 = (bf16[256,3072]{1,0:T(8,128)(2,1)}, bf16[256,3072]{1,0:T(8,128)(2,1)}, bf16[256,3072]{1,0:T(8,128)(2,1)}) custom-call(bf16[256,3072]{1,0:T(8,128)(2,1)} %q_in.1, bf16[256,3072]{1,0:T(8,128)(2,1)} %k_in.1, bf16[256,3072]{1,0:T(8,128)(2,1)} %v_in.1, bf16[256,3072]{1,0:T(8,128)(2,1)} %o_in.1, bf16[256,3072]{1,0:T(8,128)(2,1)} %g_in.1, ...), custom_call_target="tpu_custom_call" | custom-call | flops 24159191040 | bytes 12582912 | tf_op jit(solution)/shard_map/clip_attention_backward/pallas_call | solution.py:357
  129.4 0.0 copy-start.1
  129.4 2.8 %copy.13 = bf16[256,3072]{1,0:T(8,128)(2,1)} copy(bf16[256,3072]{1,0:T(8,128)(2,1)} %get-tuple-element.6) | data formatting | bytes 3145728
  132.2 0.0 copy-done.1
  132.2 0.0 copy-start
  132.2 1.1 copy.14
  133.3 0.8 copy-done
  134.2 1.1 copy.15
Async XLA Ops:
  129.4 2.8 %copy-start.1 = (bf16[256,3072]{1,0:T(8,128)(2,1)S(1)}, bf16[256,3072]{1,0:T(8,128)(2,1)}, u32[]{:S(2)}) copy-start(bf16[256,3072]{1,0:T(8,128)(2,1)} %get-tuple-element.7) | copy-start | bytes 4718596
  132.2 2.0 %copy-start = (bf16[256,3072]{1,0:T(8,128)(2,1)S(1)}, bf16[256,3072]{1,0:T(8,128)(2,1)}, u32[]{:S(2)}) copy-start(bf16[256,3072]{1,0:T(8,128)(2,1)} %get-tuple-element.8) | copy-start | bytes 4718596

commit v4 on v3

--- a/solution.py
+++ b/solution.py
@@ -15,7 +15,7 @@
 BQ = 1024
 AHEAD = 2
 HOLD = 5
-HOLD_DQ = 4
+EARLY = 3
 MESH = pl.DeviceIdType.MESH
 SCALE = HD**-0.5
 LOG2E = 1.4426950408889634
@@ -30,7 +30,7 @@
 def kernel(
     q_in, k_in, v_in, o_in, g_in, lse_in, clip_in,
     q_out, k_out, v_out,
-    qg, kv, own, dq, dq_away, dq_in, part, relay, back1, back2, stage, o_loc, g_loc, dl_src, dl, lse_far, lse3,
+    qg, kv, own, dq, dq_in, part, relay, back1, back2, stage, dl_src, dl, lse_far, lse3,
     in_send, kv_in, outer_in, q_in_sem, fwd_send, kv_send, kv_recv, part_send, relay_recv, back_recv,
     dq_send, dq_recv, out_send, out_recv, dl_send, dl_recv, loc,
 ):
@@ -67,16 +67,20 @@
     SET = (0, -1)
     NEAR, FAR = pl.ds(0, ROWS), pl.ds(ROWS, ROWS)
 
-    get_o = pltpu.make_async_copy(o_in, o_loc, loc.at[0])
-    get_g = pltpu.make_async_copy(g_in, g_loc, loc.at[1])
-    get_o.start()
-    get_g.start()
-
     barrier = pltpu.get_barrier_semaphore()
     for p in range(1, RANKS):
         pl.semaphore_signal(barrier, inc=1, device_id=at_rank(p), device_id_type=MESH)
     for d in (-2, -1, 1, 2):
         pl.semaphore_signal(barrier, inc=1, device_id=at_ctx(d), device_id_type=MESH)
+
+    def load(h, _):
+        for r in range(RANKS):
+            cols = pl.ds(pl.multiple_of((r * HEADS + h) * HD, HD), HD)
+            pltpu.make_async_copy(o_in.at[:, cols], stage.at[r // 2, h, r % 2, NEAR], loc).start()
+            pltpu.make_async_copy(g_in.at[:, cols], stage.at[r // 2, h, r % 2, FAR], loc).start()
+        return 0
+
+    lax.fori_loop(0, HEADS, load, 0)
     pl.semaphore_wait(barrier, RANKS - 1 + 4)
 
     def fetch_outer(h):
@@ -122,19 +126,16 @@
         def _():
             remote(kv.at[0, h], kv.at[2, h], kv_send.at[1, h], kv_recv.at[1, h], at_ctx(2))
 
-    for h in range(AHEAD):
-        fetch_outer(h)
-        fetch_own(h)
+    fetch_outer(0)
+    fetch_own(0)
     remote(lse_in, lse_far, dl_send.at[0], dl_recv.at[0], at_rank(1))
 
-    get_o.wait()
-    get_g.wait()
+    arrived(stage.at[pl.ds(0, 2)], loc)
     lane = lax.broadcasted_iota(jnp.int32, (ROWS, HD), 1)
     delta = jnp.zeros((ROWS, HD), f32)
     for r in range(RANKS):
         for h in range(HEADS):
-            cols = pl.ds((r * HEADS + h) * HD, HD)
-            prod = o_loc[:, cols].astype(f32) * g_loc[:, cols].astype(f32)
+            prod = stage[r // 2, h, r % 2, NEAR].astype(f32) * stage[r // 2, h, r % 2, FAR].astype(f32)
             total = jnp.sum(prod, axis=1, keepdims=True)
             delta = jnp.where(lane == r * 8 + h, total, delta)
     flipped = delta.T
@@ -148,8 +149,10 @@
             else:
                 remote(src, dst, dl_send.at[1], dl_recv.at[1], at_rank(p))
 
+    fetch_outer(1)
+    forward(0)
     give(0)
-    forward(0)
+    fetch_own(1)
 
     arrived(lse_far, dl_recv.at[0])
     here = clip_in[c]
@@ -188,9 +191,9 @@
             else:
                 part[j - 1, h, role, 0] = dk.astype(bf16)
                 part[j - 1, h, role, 1] = dv.astype(bf16)
-            return 0
-
-        lax.fori_loop(0, 2, one, 0)
+
+        one(0, 0)
+        one(1, 0)
 
     def put(which, out, h):
         for role in (0, 1):
@@ -203,12 +206,13 @@
 
     def share_dq(h):
         for role in (0, 1):
-            dq_away[h, role, NEAR] = dq[h, role, :, block(SIDE[role])].T.astype(bf16)
-            dq_away[h, role, FAR] = dq[h, role, :, block(2)].T.astype(bf16)
-            remote(dq_away.at[h, role], dq_in.at[h, 1 - role], dq_send.at[h], dq_recv.at[h], at_rank(SIDE[role]))
+            stage[0, h, role, NEAR] = dq[h, role, :, block(SIDE[role])].T.astype(bf16)
+            stage[0, h, role, FAR] = dq[h, role, :, block(2)].T.astype(bf16)
+            remote(stage.at[0, h, role], dq_in.at[h, 1 - role], dq_send.at[h], dq_recv.at[h], at_rank(SIDE[role]))
 
     def finish_dq(h):
         arrived(dq_in.at[h], dq_recv.at[h])
+        arrived(stage.at[0, h], dq_send.at[h])
         for role in (0, 1):
             for where, p in ((NEAR, 0), (FAR, -SIDE[role])):
                 total = dq[h, role, :, block(p)].T + dq_in[h, role, where].astype(f32)
@@ -237,18 +241,12 @@
         put(1, k_out, h)
         put(2, v_out, h)
 
-    def later(i, first, lag, do):
-        @pl.when(i == first)
-        def _():
-            def each(h, _):
-                do(h)
-                return 0
-
-            lax.fori_loop(0, first - lag + 1, each, 0)
-
-        @pl.when(jnp.logical_and(i > first, i - lag < HEADS))
-        def _():
-            do(i - lag)
+    def several(first, last, do):
+        def each(h, _):
+            do(h)
+            return 0
+
+        lax.fori_loop(first, last, each, 0)
 
     def step(i, _):
         @pl.when(i + AHEAD < HEADS)
@@ -258,6 +256,14 @@
         @pl.when(i < HEADS)
         def _():
             arrived(qg.at[i, :, :, pl.ds(0, GROUP - ROWS)], q_in_sem.at[i])
+
+        @pl.when(i == HOLD)
+        def _():
+            several(0, HOLD - 2, put_kv)
+            several(EARLY, HOLD - 1, share_dq)
+
+        @pl.when(i < HEADS)
+        def _():
             grads(i, 0)
 
         @pl.when(i + 1 < HEADS)
@@ -297,14 +303,25 @@
             def _():
                 remote(part.at[1, h], back2.at[h], part_send.at[1, h], back_recv.at[1, h], at_ctx(-2))
 
-        later(i, HOLD_DQ, 1, share_dq)
+        @pl.when(jnp.logical_or(i <= EARLY, i >= HOLD) & inner)
+        def _():
+            share_dq(i - 1)
 
         @pl.when(i >= 2)
         def _():
             finish_kv(i - 2)
 
-        later(i, HOLD, 2, put_kv)
-        later(i, HOLD, 2, finish_dq)
+        @pl.when(i >= HOLD)
+        def _():
+            put_kv(i - 2)
+
+        @pl.when(i == HOLD)
+        def _():
+            several(0, HOLD - 1, finish_dq)
+
+        @pl.when(i > HOLD)
+        def _():
+            finish_dq(i - 2)
 
         @pl.when(jnp.logical_and(inner, even))
         def _():
@@ -330,7 +347,6 @@
         arrived(kv.at[0, h], kv_send.at[0, h])
         arrived(part.at[0, h], part_send.at[0, h])
         arrived(part.at[1, h], part_send.at[1, h])
-        arrived(dq_away.at[h], dq_send.at[h])
         for n in range(3):
             arrived(stage.at[n, h, :, NEAR], out_send.at[n, h])
 
@@ -354,9 +370,10 @@
     dma = pltpu.SemaphoreType.DMA
     half = (HEADS, 2, 2, KEYS, HD)
     out = jax.ShapeDtypeStruct((ROWS, RANKS * HEADS * HD), bf16)
-    return pl.pallas_call(
+    near = pltpu.VMEM((ROWS, RANKS * HEADS * HD), bf16)
+    grads = pl.pallas_call(
         kernel,
-        out_shape=(out, out, out),
+        out_shape=(near, near, near),
         in_specs=[hbm, hbm, hbm, hbm, hbm, vmem, smem],
         out_specs=(hbm, hbm, hbm),
         scratch_shapes=[
@@ -365,14 +382,11 @@
             pltpu.VMEM(half, f32),
             pltpu.VMEM((HEADS, 2, HD, GROUP), f32),
             pltpu.VMEM((HEADS, 2, KEYS, HD), bf16),
-            pltpu.VMEM((HEADS, 2, KEYS, HD), bf16),
             pltpu.VMEM((2, *half), bf16),
             pltpu.VMEM(half, bf16),
             pltpu.VMEM(half, bf16),
             pltpu.VMEM(half, bf16),
             pltpu.VMEM((3, HEADS, 2, KEYS, HD), bf16),
-            pltpu.VMEM((ROWS, RANKS * HEADS * HD), bf16),
-            pltpu.VMEM((ROWS, RANKS * HEADS * HD), bf16),
             pltpu.VMEM((RANKS, 8, ROWS), f32),
             pltpu.VMEM((2, 8, GROUP), f32),
             pltpu.VMEM((HEADS, GROUP), f32),
@@ -393,7 +407,7 @@
             dma((3,)),
             dma((2,)),
             dma((2,)),
-            dma((2,)),
+            dma,
         ],
         cost_estimate=pl.CostEstimate(
             flops=2 * 5 * 3 * HEADS * GROUP * GROUP * HD,
@@ -401,10 +415,12 @@
             transcendentals=3 * HEADS * GROUP * GROUP,
         ),
         compiler_params=pltpu.CompilerParams(
-            collective_id=0, has_side_effects=True, vmem_limit_bytes=60 * 2**20
+            collective_id=0, has_side_effects=True, vmem_limit_bytes=53 * 2**20
         ),
         name="clip_attention_backward",
     )(queries, keys, values, outputs, out_grad, logsumexp, clip_of_group)
+
+    return grads
 
 
 def solution(mesh):

time: 136 us -> 132 us (0.971)
  local copies, waits for them, and re-layouts: 5.89 us -> 3.43 us
  Pallas kernels: 129 us -> 127 us
    unnamed x7 -> x3, local copies, waits for them, and re-layouts: 5.89 us -> 3.43 us
    pallas_call x1, Pallas kernels: 129 us -> 127 us  [local(): pl.pallas_call(kernel, out_shape=(near, near, near), in_specs=[hbm, hbm,...]
where the time goes in v4:
time: 132 us; the launch traced here: 131 us
  Pallas kernels  127 us (96%)
  local copies, waits for them, and re-layouts  3.43 us (3%)
    pallas_call x1, Pallas kernels, local(): pl.pallas_call(kernel, out_shape=(near, near, near), in_specs=[hbm, hbm,...  127 us
    unnamed x3, local copies, waits for them, and re-layouts  3.43 us

profile of v4, /device:TPU:1, one launch (start us, length us, event | category | flops | bytes accessed | tf_op | source)
XLA Modules:
  0.0 130.9 jit_solution(7190636535640657457)
XLA Ops:
  0.6 126.8 %clip_attention_backward.1 = (bf16[256,3072]{1,0:T(8,128)(2,1)S(1)}, bf16[256,3072]{1,0:T(8,128)(2,1)S(1)}, bf16[256,3072]{1,0:T(8,128)(2,1)S(1)}) custom-call(bf16[256,3072]{1,0:T(8,128)(2,1)} %q_in.1, bf16[256,3072]{1,0:T(8,128)(2,1)} %k_in.1, bf16[256,3072]{1,0:T(8,128)(2,1)} %v_in.1, bf16[256,3072]{1,0:T(8,128)(2,1)} %o_in.1, bf16[256,3072]{1,0:T(8,128)(2,1)} %g_in.1, ...), custom_call_target="tpu_custom_call" | custom-call | flops 24159191040 | bytes 12582912 | tf_op jit(solution)/shard_map/clip_attention_backward/pallas_call | solution.py:374
  127.5 1.1 copy.13
  128.6 1.1 copy.14
  129.8 1.1 copy.15

commit v5 on v4

--- a/solution.py
+++ b/solution.py
@@ -89,6 +89,8 @@
             cols = head_cols(side + SET[role], h)
             for n, src in ((0, q_in), (1, g_in)):
                 remote(src.at[:, cols], qg.at[h, role, n, block(0)], in_send.at[h], outer_in.at[h], at_rank(side))
+
+    def fetch_kv(h):
         for role in (0, 1):
             side = SIDE[role]
             cols = head_cols(side + SET[role], h)
@@ -126,8 +128,10 @@
         def _():
             remote(kv.at[0, h], kv.at[2, h], kv_send.at[1, h], kv_recv.at[1, h], at_ctx(2))
 
+    fetch_kv(0)
     fetch_outer(0)
     fetch_own(0)
+    fetch_kv(1)
     remote(lse_in, lse_far, dl_send.at[0], dl_recv.at[0], at_rank(1))
 
     arrived(stage.at[pl.ds(0, 2)], loc)
@@ -153,6 +157,8 @@
     forward(0)
     give(0)
     fetch_own(1)
+    fetch_kv(2)
+    give(1)
 
     arrived(lse_far, dl_recv.at[0])
     here = clip_in[c]
@@ -253,6 +259,10 @@
         def _():
             fetch_outer(i + AHEAD)
 
+        @pl.when(i + AHEAD + 1 < HEADS)
+        def _():
+            fetch_kv(i + AHEAD + 1)
+
         @pl.when(i < HEADS)
         def _():
             arrived(qg.at[i, :, :, pl.ds(0, GROUP - ROWS)], q_in_sem.at[i])
@@ -260,32 +270,35 @@
         @pl.when(i == HOLD)
         def _():
             several(0, HOLD - 2, put_kv)
-            several(EARLY, HOLD - 1, share_dq)
+            several(EARLY, HOLD, share_dq)
 
         @pl.when(i < HEADS)
         def _():
-            grads(i, 0)
-
-        @pl.when(i + 1 < HEADS)
-        def _():
-            give(i + 1)
-            forward(i + 1)
-
-        @pl.when(i + AHEAD < HEADS)
-        def _():
-            fetch_own(i + AHEAD)
-
-        inner = jnp.logical_and(i >= 1, i <= HEADS)
-
-        @pl.when(inner)
-        def _():
-            h = i - 1
-            arrived(kv.at[1, h], kv_recv.at[0, h])
+            arrived(kv.at[1, i], kv_recv.at[0, i])
 
             @pl.when(even)
             def _():
-                remote(kv.at[1, h], kv.at[2, h], kv_send.at[2, h], kv_recv.at[1, h], at_ctx(1))
-
+                remote(kv.at[1, i], kv.at[2, i], kv_send.at[2, i], kv_recv.at[1, i], at_ctx(1))
+
+            grads(i, 0)
+
+        @pl.when(i + 1 < HEADS)
+        def _():
+            forward(i + 1)
+
+        @pl.when(i + 2 < HEADS)
+        def _():
+            give(i + 2)
+
+        @pl.when(i + AHEAD < HEADS)
+        def _():
+            fetch_own(i + AHEAD)
+
+        inner = i < HEADS
+
+        @pl.when(inner)
+        def _():
+            h = i
             grads(h, 1)
 
             @pl.when(odd)
@@ -303,35 +316,39 @@
             def _():
                 remote(part.at[1, h], back2.at[h], part_send.at[1, h], back_recv.at[1, h], at_ctx(-2))
 
-        @pl.when(jnp.logical_or(i <= EARLY, i >= HOLD) & inner)
-        def _():
-            share_dq(i - 1)
-
-        @pl.when(i >= 2)
-        def _():
-            finish_kv(i - 2)
-
-        @pl.when(i >= HOLD)
-        def _():
-            put_kv(i - 2)
-
-        @pl.when(i == HOLD)
-        def _():
-            several(0, HOLD - 1, finish_dq)
-
-        @pl.when(i > HOLD)
-        def _():
-            finish_dq(i - 2)
-
         @pl.when(jnp.logical_and(inner, even))
         def _():
-            h = i - 1
+            h = i
             arrived(relay.at[h], relay_recv.at[h])
             for role in (0, 1):
                 for n in (0, 1):
                     total = part[0, h, role, n].astype(f32) + relay[h, role, n].astype(f32)
                     part[0, h, role, n] = total.astype(bf16)
             remote(part.at[0, h], back1.at[h], part_send.at[0, h], back_recv.at[0, h], at_ctx(-1))
+
+        @pl.when(jnp.logical_and(i >= 1, i <= EARLY))
+        def _():
+            share_dq(i - 1)
+
+        @pl.when(i == HOLD)
+        def _():
+            share_dq(HOLD)
+
+        @pl.when(i >= 2)
+        def _():
+            finish_kv(i - 2)
+
+        @pl.when(i >= HOLD)
+        def _():
+            put_kv(i - 2)
+
+        @pl.when(i == HOLD)
+        def _():
+            several(0, HOLD - 1, finish_dq)
+
+        @pl.when(i > HOLD)
+        def _():
+            finish_dq(i - 2)
 
         return 0
 

time: 132 us -> 128 us (0.970)
  Pallas kernels: 127 us -> 122 us
    pallas_call x1, Pallas kernels: 127 us -> 122 us  [local(): pl.pallas_call(kernel, out_shape=(near, near, near), in_specs=[hbm, hbm,...]
where the time goes in v5:
time: 128 us; the launch traced here: 126 us
  Pallas kernels  122 us (95%)
  local copies, waits for them, and re-layouts  3.43 us (3%)
    pallas_call x1, Pallas kernels, local(): pl.pallas_call(kernel, out_shape=(near, near, near), in_specs=[hbm, hbm,...  122 us
    unnamed x3, local copies, waits for them, and re-layouts  3.43 us

profile of v5, /device:TPU:1, one launch (start us, length us, event | category | flops | bytes accessed | tf_op | source)
XLA Modules:
  0.0 126.1 jit_solution(11324714096943919415)
XLA Ops:
  0.6 122.1 %clip_attention_backward.1 = (bf16[256,3072]{1,0:T(8,128)(2,1)S(1)}, bf16[256,3072]{1,0:T(8,128)(2,1)S(1)}, bf16[256,3072]{1,0:T(8,128)(2,1)S(1)}) custom-call(bf16[256,3072]{1,0:T(8,128)(2,1)} %q_in.1, bf16[256,3072]{1,0:T(8,128)(2,1)} %k_in.1, bf16[256,3072]{1,0:T(8,128)(2,1)} %v_in.1, bf16[256,3072]{1,0:T(8,128)(2,1)} %o_in.1, bf16[256,3072]{1,0:T(8,128)(2,1)} %g_in.1, ...), custom_call_target="tpu_custom_call" | custom-call | flops 24159191040 | bytes 12582912 | tf_op jit(solution)/shard_map/clip_attention_backward/pallas_call | solution.py:391
  122.7 1.1 copy.13
  123.8 1.1 copy.14
  125.0 1.1 copy.15

commit v6 on v5

--- a/solution.py
+++ b/solution.py
@@ -15,7 +15,7 @@
 BQ = 1024
 AHEAD = 2
 HOLD = 5
-EARLY = 3
+EARLY = 4
 MESH = pl.DeviceIdType.MESH
 SCALE = HD**-0.5
 LOG2E = 1.4426950408889634
@@ -330,9 +330,9 @@
         def _():
             share_dq(i - 1)
 
-        @pl.when(i == HOLD)
-        def _():
-            share_dq(HOLD)
+        @pl.when(jnp.logical_and(i >= HOLD, i < HEADS))
+        def _():
+            share_dq(i)
 
         @pl.when(i >= 2)
         def _():
@@ -437,7 +437,22 @@
         name="clip_attention_backward",
     )(queries, keys, values, outputs, out_grad, logsumexp, clip_of_group)
 
-    return grads
+    def write(*refs):
+        copies = [pltpu.make_async_copy(refs[n], refs[3 + n], refs[6].at[n]) for n in range(3)]
+        for copy in copies:
+            copy.start()
+        for copy in copies:
+            copy.wait()
+
+    return pl.pallas_call(
+        write,
+        out_shape=(out,) * 3,
+        in_specs=[hbm] * 3,
+        out_specs=(hbm,) * 3,
+        scratch_shapes=[dma((3,))],
+        compiler_params=pltpu.CompilerParams(vmem_limit_bytes=4 * 2**20),
+        name="write_out",
+    )(*(pltpu.with_memory_space_constraint(grad, pltpu.VMEM) for grad in grads))
 
 
 def solution(mesh):

time: 128 us -> 126 us (0.984)
  local copies, waits for them, and re-layouts: 3.43 us -> 0 us
    unnamed x3 -> x0, local copies, waits for them, and re-layouts: 3.43 us -> none
    pallas_call x0 -> x1, Pallas kernels: none -> 2.21 us  [local(): pl.pallas_call(write, out_shape=(out,) * 3, in_specs=[hbm] * 3, out_specs...]
where the time goes in v6:
time: 126 us; the launch traced here: 124 us
  Pallas kernels  123 us (98%)
    pallas_call x1, Pallas kernels, local(): pl.pallas_call(kernel, out_shape=(near, near, near), in_specs=[hbm, hbm,...  121 us

profile of v6, /device:TPU:1, one launch (start us, length us, event | category | flops | bytes accessed | tf_op | source)
XLA Modules:
  0.0 124.0 jit_solution(17371712884608155612)
XLA Ops:
  0.6 121.1 %clip_attention_backward.1 = (bf16[256,3072]{1,0:T(8,128)(2,1)S(1)}, bf16[256,3072]{1,0:T(8,128)(2,1)S(1)}, bf16[256,3072]{1,0:T(8,128)(2,1)S(1)}) custom-call(bf16[256,3072]{1,0:T(8,128)(2,1)} %q_in.1, bf16[256,3072]{1,0:T(8,128)(2,1)} %k_in.1, bf16[256,3072]{1,0:T(8,128)(2,1)} %v_in.1, bf16[256,3072]{1,0:T(8,128)(2,1)} %o_in.1, bf16[256,3072]{1,0:T(8,128)(2,1)} %g_in.1, ...), custom_call_target="tpu_custom_call" | custom-call | flops 24159191040 | bytes 12582912 | tf_op jit(solution)/shard_map/clip_attention_backward/pallas_call | solution.py:391
  121.8 2.2 %write_out.1 = (bf16[256,3072]{1,0:T(8,128)(2,1)}, bf16[256,3072]{1,0:T(8,128)(2,1)}, bf16[256,3072]{1,0:T(8,128)(2,1)}) custom-call(bf16[256,3072]{1,0:T(8,128)(2,1)S(1)} %get-tuple-element.6.refs_0_, bf16[256,3072]{1,0:T(8,128)(2,1)S(1)} %get-tuple-element.7.refs_1_, bf16[256,3072]{1,0:T(8,128)(2,1)S(1)} %get-tuple-element.8.refs_2_), custom_call_target="tpu_custom_call" | custom-call | tf_op jit(solution)/shard_map/write_out/pallas_call | solution.py:447
